TPU v7x, 32 devices: a whole 2x2x4 slice. The times are simulated.
32 devices in a mesh: grp: 2 (over x), seq: 16 (over z, y, core).
Axes of the slice: x: 2, y: 2, z: 4, core: 2. Of those that a mesh axis runs over, the one named last changes fastest.
Arguments:
- queries: bfloat16 [4096, 64, 128], P(('grp', 'seq')), parts along dimension 0, may hold values from -216 to 216
- window_keys: bfloat16 [4096, 8, 128], P(('grp', 'seq')), parts along dimension 0, may hold values from -6 to 6
- window_values: bfloat16 [4096, 8, 128], P(('grp', 'seq')), parts along dimension 0, may hold values from -6 to 6
- cache_keys: bfloat16 [8192, 8, 128], P(('grp', 'seq')), parts along dimension 0, may hold values from -6 to 6
- cache_values: bfloat16 [8192, 8, 128], P(('grp', 'seq')), parts along dimension 0, may hold values from -6 to 6
- vertical_blocks: int32 [128, 4], P('grp'), parts along dimension 0, may hold values from 0 to 63, as said below
- slash_offsets: int32 [128, 12], P('grp'), parts along dimension 0, may hold values from 0 to 31, as said below
Outputs:
- attended: bfloat16 [4096, 64, 128], P(('grp', 'seq')), parts along dimension 0
There are 2 independent parts, one for each index of `grp`. A program takes and returns all parts, laid end to end along the dimension named above; each array names one. Nothing has to cross between parts.
Inputs may be any that keep to these rules, and one draw needn't show every extreme that they name: `vertical_blocks`: the 4 entries of a head are distinct and lie in 4 different runs of 4 consecutive blocks (block b lies in run b // 4). `slash_offsets`: the 12 entries of a head are distinct, and one of them is 0.
All inputs are finite; a program needn't handle non-finite values.
Results may differ from a plain program's by a relative error of at most 0.0046.
Values may be sent and summed in bfloat16 or wider, within the bound.
A program may use at most 128 MiB of HBM per device.

v0:
```python
import math

import jax
import jax.numpy as jnp
from jax import lax
from jax.sharding import PartitionSpec as P

BLOCK = 64


def attend_head(queries, key_rows, values, column_keys, column_values, offsets):
    head_dim = queries.shape[-1]
    blocks = queries.shape[0] // BLOCK
    per_step = math.gcd(512 // BLOCK, blocks)
    query_blocks = queries.reshape(blocks, BLOCK, head_dim)
    key_blocks = key_rows.reshape(blocks, BLOCK, head_dim)
    value_blocks = values.reshape(blocks, BLOCK, head_dim)
    column_flat = column_keys.reshape(-1, head_dim)
    column_vals = column_values.reshape(-1, head_dim)
    factor = 1.0 / math.sqrt(head_dim)
    places = jnp.arange(BLOCK, dtype=jnp.int32)
    earlier = places[None, :] <= places[:, None]
    open_slash = offsets != 0

    def one_step(first_block):
        block_ids = first_block + jnp.arange(per_step, dtype=jnp.int32)
        sources = block_ids[:, None] - offsets[None, :]
        usable = sources >= 0
        safe_ids = jnp.maximum(sources, 0)
        query_group = lax.dynamic_slice_in_dim(query_blocks, first_block, per_step, 0)
        slash_keys = key_blocks[safe_ids].reshape(per_step, -1, head_dim)
        slash_values = value_blocks[safe_ids].reshape(per_step, -1, head_dim)
        slash_scores = (
            jnp.einsum("gqd,gkd->gqk", query_group, slash_keys, preferred_element_type=jnp.float32)
            * factor
        )
        column_scores = (
            jnp.dot(
                query_group.reshape(-1, head_dim), column_flat.T, preferred_element_type=jnp.float32
            ).reshape(per_step, BLOCK, -1)
            * factor
        )
        keep = usable[:, None, :, None] & (
            open_slash[None, None, :, None] | earlier[None, :, None, :]
        )
        keep = keep.reshape(per_step, BLOCK, -1)
        slash_scores = jnp.where(keep, slash_scores, -1e30)
        highest = jnp.maximum(jnp.max(slash_scores, axis=-1), jnp.max(column_scores, axis=-1))
        slash_weights = jnp.exp(slash_scores - highest[..., None])
        column_weights = jnp.exp(column_scores - highest[..., None])
        total = jnp.sum(slash_weights, axis=-1) + jnp.sum(column_weights, axis=-1)
        slash_low = slash_weights.astype(jnp.bfloat16)
        column_low = column_weights.astype(jnp.bfloat16)
        mixed = jnp.einsum(
            "gqk,gkd->gqd", slash_low, slash_values, preferred_element_type=jnp.float32
        )
        mixed = mixed + jnp.dot(
            column_low.reshape(-1, column_low.shape[-1]),
            column_vals,
            preferred_element_type=jnp.float32,
        ).reshape(per_step, BLOCK, head_dim)
        return (mixed / total[..., None]).astype(jnp.bfloat16)

    starts = jnp.arange(0, blocks, per_step, dtype=jnp.int32)
    result = lax.map(one_step, starts)
    return result.reshape(-1, head_dim)


def body(
    queries, window_keys, window_values, cache_keys, cache_values, vertical_blocks, slash_offsets
):
    head_count = queries.shape[1]
    head_dim = queries.shape[2]
    group_heads = window_keys.shape[1]
    repeat_count = head_count // group_heads
    seq_devices = lax.axis_size("seq")
    per_dev = head_count // seq_devices
    first_head = lax.axis_index("seq") * per_dev
    wide_keys = jnp.repeat(window_keys, repeat_count, axis=1)
    wide_values = jnp.repeat(window_values, repeat_count, axis=1)
    head_queries, head_keys, head_values = (
        lax.all_to_all(queries, "seq", split_axis=1, concat_axis=0, tiled=True),
        lax.all_to_all(wide_keys, "seq", split_axis=1, concat_axis=0, tiled=True),
        lax.all_to_all(wide_values, "seq", split_axis=1, concat_axis=0, tiled=True),
    )
    my_columns = lax.dynamic_slice_in_dim(vertical_blocks, first_head, per_dev, 0)
    my_offsets = lax.dynamic_slice_in_dim(slash_offsets, first_head, per_dev, 0)
    cache_wide_keys = jnp.repeat(cache_keys, repeat_count, axis=1)
    cache_wide_values = jnp.repeat(cache_values, repeat_count, axis=1)
    full_keys, full_values = (
        lax.all_to_all(cache_wide_keys, "seq", split_axis=1, concat_axis=0, tiled=True),
        lax.all_to_all(cache_wide_values, "seq", split_axis=1, concat_axis=0, tiled=True),
    )
    key_layout = full_keys.reshape(-1, BLOCK, per_dev, head_dim)
    value_layout = full_values.reshape(-1, BLOCK, per_dev, head_dim)
    head_slots = jnp.arange(per_dev, dtype=jnp.int32)[:, None]
    column_keys = key_layout[my_columns, :, head_slots]
    column_values = value_layout[my_columns, :, head_slots]

    def per_head(member):
        return attend_head(member[0], member[1], member[2], member[3], member[4], member[5])

    stacked = (
        jnp.moveaxis(head_queries, 1, 0),
        jnp.moveaxis(head_keys, 1, 0),
        jnp.moveaxis(head_values, 1, 0),
        column_keys,
        column_values,
        my_offsets,
    )
    outputs = lax.map(per_head, stacked)
    by_position = jnp.moveaxis(outputs, 0, 1)
    return lax.all_to_all(by_position, "seq", split_axis=0, concat_axis=1, tiled=True)


def solution(mesh):
    placed = (
        P(("grp", "seq"), None, None),
        P(("grp", "seq"), None, None),
        P(("grp", "seq"), None, None),
        P(("grp", "seq"), None, None),
        P(("grp", "seq"), None, None),
        P("grp", None),
        P("grp", None),
    )
    return jax.shard_map(
        body, mesh=mesh, in_specs=placed, out_specs=P(("grp", "seq"), None, None), check_vma=False
    )
```

profile of v0, /device:TPU:1, one launch (start us, length us, event | category | flops | bytes accessed | tf_op | source)
XLA Modules:
  0.0 680.5 jit_solution(14727938756555138328)
XLA Ops:
  2.8 7.5 %all-to-all-start.1 = ((bf16[128,64,128]{2,0,1:T(8,128)(2,1)}), bf16[128,64,128]{2,0,1:T(8,128)(2,1)S(1)}, u32[]{:S(2)}, u32[]{:S(2)}) async-start(bf16[128,64,128]{2,0,1:T(8,128)(2,1)} %bitcast.109), calls=%async_computation.1 | async-start | bytes 4194304 | tf_op jit(solution)/shard_map/all_to_all | solution.py:83
  10.4 41.4 %all-to-all-done.1 = bf16[128,64,128]{2,0,1:T(8,128)(2,1)S(1)} async-done(((bf16[128,64,128]{2,0,1:T(8,128)(2,1)}), bf16[128,64,128]{2,0,1:T(8,128)(2,1)S(1)}, u32[]{:S(2)}, u32[]{:S(2)}) %all-to-all-start.1) | async-done | bytes 2097184 | tf_op jit(solution)/shard_map/all_to_all | solution.py:83
  53.6 10.9 %all-to-all-start.2 = ((bf16[128,64,128]{2,0,1:T(8,128)(2,1)}), bf16[128,64,128]{2,0,1:T(8,128)(2,1)}, u32[]{:S(2)}, u32[]{:S(2)}) async-start(bf16[128,64,128]{2,0,1:T(8,128)(2,1)} %bitcast.110), calls=%async_computation.2 | async-start | bytes 4194304 | tf_op jit(solution)/shard_map/all_to_all | solution.py:84
  64.5 4.3 copy.35
  68.8 37.3 %all-to-all-done.2 = bf16[128,64,128]{2,0,1:T(8,128)(2,1)} async-done(((bf16[128,64,128]{2,0,1:T(8,128)(2,1)}), bf16[128,64,128]{2,0,1:T(8,128)(2,1)}, u32[]{:S(2)}, u32[]{:S(2)}) %all-to-all-start.2) | async-done | bytes 2097184 | tf_op jit(solution)/shard_map/all_to_all | solution.py:84
  106.1 10.9 %all-to-all-start = ((bf16[128,64,128]{2,0,1:T(8,128)(2,1)}), bf16[128,64,128]{2,0,1:T(8,128)(2,1)}, u32[]{:S(2)}, u32[]{:S(2)}) async-start(bf16[128,64,128]{2,0,1:T(8,128)(2,1)} %copy.35), calls=%async_computation | async-start | bytes 4194304 | tf_op jit(solution)/shard_map/all_to_all | solution.py:82
  117.0 41.5 %all-to-all-done = bf16[128,64,128]{2,0,1:T(8,128)(2,1)} async-done(((bf16[128,64,128]{2,0,1:T(8,128)(2,1)}), bf16[128,64,128]{2,0,1:T(8,128)(2,1)}, u32[]{:S(2)}, u32[]{:S(2)}) %all-to-all-start) | async-done | bytes 2097184 | tf_op jit(solution)/shard_map/all_to_all | solution.py:82
  158.5 3.1 broadcast_in_dim.27
  161.6 11.0 %all-to-all-start.3 = ((bf16[256,64,128]{2,0,1:T(8,128)(2,1)}), bf16[256,64,128]{2,0,1:T(8,128)(2,1)}, u32[]{:S(2)}, u32[]{:S(2)}) async-start(bf16[256,64,128]{2,0,1:T(8,128)(2,1)} %bitcast.105), calls=%async_computation.3 | async-start | bytes 8388608 | tf_op jit(solution)/shard_map/all_to_all | solution.py:91
  172.7 78.0 %all-to-all-done.3 = bf16[256,64,128]{2,0,1:T(8,128)(2,1)} async-done(((bf16[256,64,128]{2,0,1:T(8,128)(2,1)}), bf16[256,64,128]{2,0,1:T(8,128)(2,1)}, u32[]{:S(2)}, u32[]{:S(2)}) %all-to-all-start.3) | async-done | bytes 4194336 | tf_op jit(solution)/shard_map/all_to_all | solution.py:91
  250.7 3.1 broadcast_in_dim.58
  253.7 19.4 %all-to-all-start.4 = ((bf16[256,64,128]{2,0,1:T(8,128)(2,1)}), bf16[256,64,128]{2,0,1:T(8,128)(2,1)}, u32[]{:S(2)}, u32[]{:S(2)}) async-start(bf16[256,64,128]{2,0,1:T(8,128)(2,1)} %bitcast.104), calls=%async_computation.4 | async-start | bytes 8388608 | tf_op jit(solution)/shard_map/all_to_all | solution.py:92
  275.1 3.1 copy.40
  278.2 3.2 copy.36
  281.4 2.5 copy.42
  283.8 2.9 copy.44
  286.7 64.5 %all-to-all-done.4 = bf16[256,64,128]{2,0,1:T(8,128)(2,1)} async-done(((bf16[256,64,128]{2,0,1:T(8,128)(2,1)}), bf16[256,64,128]{2,0,1:T(8,128)(2,1)}, u32[]{:S(2)}, u32[]{:S(2)}) %all-to-all-start.4) | async-done | bytes 4194336 | tf_op jit(solution)/shard_map/all_to_all | solution.py:92
  351.2 2.5 copy.46
  353.7 2.9 copy.47
  356.6 3.5 gather_fusion.2
  360.1 3.5 gather_fusion.3
  363.6 244.1 %while.22 = (s32[]{:T(128)}, bf16[4,2048,128]{2,1,0:T(8,128)(2,1)}, s32[4,12]{1,0:T(4,128)S(1)}, bf16[4,2048,128]{2,1,0:T(8,128)(2,1)}, bf16[4,2048,128]{2,1,0:T...) while((s32[]{:T(128)}, bf16[4,2048,128]{2,1,0:T(8,128)(2,1)}, ...), condition=%wide.region_7.8_spmd, body=%wide.region_0.7_spmd.sunk | while | flops 272617888 | bytes 25797876 | solution.py:111
  363.6 2.3 constant_dynamic-slice_fusion.11
  368.7 54.1 %while.23 = (s32[]{:T(128)}, bf16[4,8,64,128]{3,2,1,0:T(8,128)(2,1)}, s32[4]{0:T(128)S(1)}, s32[12]{0:T(128)S(1)}, pred[12]{0:T(512)(128)(4,1)S(1)}, /*index=5*/...) while((s32[]{:T(128)}, ...), condition=%wide.region_6.6_spmd.clone, body=%wide.region_1.5_spmd.clone.sunk | while | flops 272617856 | bytes 21340540 | solution.py:65
  372.0 1.9 gather_fusion.1
  385.5 1.9 gather_fusion.1
  399.1 1.9 gather_fusion.1
  412.6 1.9 gather_fusion.1
  424.7 2.3 constant_dynamic-slice_fusion.11
  429.7 54.1 %while.23 = (s32[]{:T(128)}, bf16[4,8,64,128]{3,2,1,0:T(8,128)(2,1)}, s32[4]{0:T(128)S(1)}, s32[12]{0:T(128)S(1)}, pred[12]{0:T(512)(128)(4,1)S(1)}, /*index=5*/...) while((s32[]{:T(128)}, ...), condition=%wide.region_6.6_spmd.clone, body=%wide.region_1.5_spmd.clone.sunk | while | flops 272617856 | bytes 21340540 | solution.py:65
  433.0 1.9 gather_fusion.1
  446.6 1.9 gather_fusion.1
  460.1 1.9 gather_fusion.1
  473.6 1.9 gather_fusion.1
  485.7 2.3 constant_dynamic-slice_fusion.11
  490.7 54.1 %while.23 = (s32[]{:T(128)}, bf16[4,8,64,128]{3,2,1,0:T(8,128)(2,1)}, s32[4]{0:T(128)S(1)}, s32[12]{0:T(128)S(1)}, pred[12]{0:T(512)(128)(4,1)S(1)}, /*index=5*/...) while((s32[]{:T(128)}, ...), condition=%wide.region_6.6_spmd.clone, body=%wide.region_1.5_spmd.clone.sunk | while | flops 272617856 | bytes 21340540 | solution.py:65
  494.1 1.9 gather_fusion.1
  507.6 1.9 gather_fusion.1
  521.1 1.9 gather_fusion.1
  534.6 1.9 gather_fusion.1
  546.7 2.3 constant_dynamic-slice_fusion.11
  551.8 54.1 %while.23 = (s32[]{:T(128)}, bf16[4,8,64,128]{3,2,1,0:T(8,128)(2,1)}, s32[4]{0:T(128)S(1)}, s32[12]{0:T(128)S(1)}, pred[12]{0:T(512)(128)(4,1)S(1)}, /*index=5*/...) while((s32[]{:T(128)}, ...), condition=%wide.region_6.6_spmd.clone, body=%wide.region_1.5_spmd.clone.sunk | while | flops 272617856 | bytes 21340540 | solution.py:65
  555.1 1.9 gather_fusion.1
  568.6 1.9 gather_fusion.1
  582.1 1.9 gather_fusion.1
  607.7 3.4 copy.52
  611.2 66.8 %all_to_all.102 = bf16[2048,4,128]{2,1,0:T(4,128)(2,1)S(1)} all-to-all(bf16[2048,4,128]{2,1,0:T(4,128)(2,1)S(1)} %bitcast.111), channel_id=1, replica_groups=mesh['grp'=2,'seq'=16] {'seq'}, dimensions={0} | all-to-all | bytes 4194304 | tf_op jit(solution)/shard_map/all_to_all | solution.py:113
  677.9 2.5 copy.49
  (483 shorter events, 180.9 us)
Async XLA Ops:
  0.0 273.4 %copy-start = (s32[64,12]{0,1:T(8,128)S(1)}, s32[64,12]{0,1:T(8,128)}, u32[]{:S(2)}) copy-start(s32[64,12]{0,1:T(8,128)} %param.17) | copy-start | bytes 9220
  2.8 7.5 %copy-start.6 = (bf16[128,8,128]{2,1,0:T(8,128)(2,1)S(1)}, bf16[128,8,128]{2,1,0:T(8,128)(2,1)}, u32[]{:S(2)}) copy-start(bf16[128,8,128]{2,1,0:T(8,128)(2,1)} %param.13) | copy-start | bytes 786436
  2.8 48.9 %all-to-all-start.1 = ((bf16[128,64,128]{2,0,1:T(8,128)(2,1)}), bf16[128,64,128]{2,0,1:T(8,128)(2,1)S(1)}, u32[]{:S(2)}, u32[]{:S(2)}) async-start(bf16[128,64,128]{2,0,1:T(8,128)(2,1)} %bitcast.109), calls=%async_computation.1 | async-start | bytes 4194304 | tf_op jit(solution)/shard_map/all_to_all | solution.py:83
  53.6 52.4 %all-to-all-start.2 = ((bf16[128,64,128]{2,0,1:T(8,128)(2,1)}), bf16[128,64,128]{2,0,1:T(8,128)(2,1)}, u32[]{:S(2)}, u32[]{:S(2)}) async-start(bf16[128,64,128]{2,0,1:T(8,128)(2,1)} %bitcast.110), calls=%async_computation.2 | async-start | bytes 4194304 | tf_op jit(solution)/shard_map/all_to_all | solution.py:84
  68.8 48.2 %copy-start.4 = (bf16[256,8,128]{2,1,0:T(8,128)(2,1)S(1)}, bf16[256,8,128]{2,1,0:T(8,128)(2,1)}, u32[]{:S(2)}) copy-start(bf16[256,8,128]{2,1,0:T(8,128)(2,1)} %param.14) | copy-start | bytes 1572868
  106.1 52.4 %all-to-all-start = ((bf16[128,64,128]{2,0,1:T(8,128)(2,1)}), bf16[128,64,128]{2,0,1:T(8,128)(2,1)}, u32[]{:S(2)}, u32[]{:S(2)}) async-start(bf16[128,64,128]{2,0,1:T(8,128)(2,1)} %copy.35), calls=%async_computation | async-start | bytes 4194304 | tf_op jit(solution)/shard_map/all_to_all | solution.py:82
  161.6 11.0 %copy-start.5 = (bf16[256,8,128]{2,1,0:T(8,128)(2,1)S(1)}, bf16[256,8,128]{2,1,0:T(8,128)(2,1)}, u32[]{:S(2)}) copy-start(bf16[256,8,128]{2,1,0:T(8,128)(2,1)} %param.15) | copy-start | bytes 1572868
  161.6 89.1 %all-to-all-start.3 = ((bf16[256,64,128]{2,0,1:T(8,128)(2,1)}), bf16[256,64,128]{2,0,1:T(8,128)(2,1)}, u32[]{:S(2)}, u32[]{:S(2)}) async-start(bf16[256,64,128]{2,0,1:T(8,128)(2,1)} %bitcast.105), calls=%async_computation.3 | async-start | bytes 8388608 | tf_op jit(solution)/shard_map/all_to_all | solution.py:91
  253.7 19.4 %copy-start.7 = (s32[64,4]{0,1:T(4,128)S(1)}, s32[64,4]{0,1:T(4,128)}, u32[]{:S(2)}) copy-start(s32[64,4]{0,1:T(4,128)} %param.16) | copy-start | bytes 3076
  253.7 97.5 %all-to-all-start.4 = ((bf16[256,64,128]{2,0,1:T(8,128)(2,1)}), bf16[256,64,128]{2,0,1:T(8,128)(2,1)}, u32[]{:S(2)}, u32[]{:S(2)}) async-start(bf16[256,64,128]{2,0,1:T(8,128)(2,1)} %bitcast.104), calls=%async_computation.4 | async-start | bytes 8388608 | tf_op jit(solution)/shard_map/all_to_all | solution.py:92
  377.5 0.8 copy-start.2
  380.2 1.0 copy-start.3
  391.1 0.8 copy-start.2
  393.8 1.0 copy-start.3
  404.6 0.8 copy-start.2
  407.3 1.0 copy-start.3
  418.1 0.8 copy-start.2
  420.8 1.0 copy-start.3
  438.6 0.8 copy-start.2
  441.3 1.0 copy-start.3
  452.1 0.8 copy-start.2
  454.8 1.0 copy-start.3
  465.6 0.8 copy-start.2
  468.3 1.0 copy-start.3
  479.1 0.8 copy-start.2
  481.8 1.0 copy-start.3
  499.6 0.8 copy-start.2
  502.3 1.0 copy-start.3
  513.1 0.8 copy-start.2
  515.8 1.0 copy-start.3
  526.6 0.8 copy-start.2
  529.3 1.0 copy-start.3
  540.2 0.8 copy-start.2
  542.9 1.0 copy-start.3
  560.6 0.8 copy-start.2
  563.3 1.0 copy-start.3
  574.1 0.8 copy-start.2
  576.8 1.0 copy-start.3
  587.7 0.8 copy-start.2
  590.4 1.0 copy-start.3
  601.2 0.8 copy-start.2
  603.9 1.0 copy-start.3
  677.9 2.5 copy-start.1
where the time goes:
time: 685 us; the launch traced here: 680 us
  waiting for transfers between devices  263 us (38%)
  local copies, waits for them, and re-layouts  165 us (24%)
  matrix products  68.9 us (10%)
  blocking collectives  66.8 us (10%)
  starting transfers between devices  59.6 us (9%)
  loops' own time  32.5 us (5%)
  other arithmetic  24.9 us (4%)
    all_to_all x1, waiting for transfers between devices, body(): lax.all_to_all(cache_wide_keys, 'seq', split_axis=1, concat_axis=0, tiled...  78 us
    all_to_all x1, blocking collectives, body(): lax.all_to_all(by_position, 'seq', split_axis=0, concat_axis=1, tiled=True)  66.8 us
    all_to_all x1, waiting for transfers between devices, body(): lax.all_to_all(cache_wide_values, 'seq', split_axis=1, concat_axis=0, til...  64.5 us
    all_to_all x1, waiting for transfers between devices, body(): lax.all_to_all(queries, 'seq', split_axis=1, concat_axis=0, tiled=True)  41.5 us
    all_to_all x1, waiting for transfers between devices, body(): lax.all_to_all(wide_keys, 'seq', split_axis=1, concat_axis=0, tiled=True)  41.4 us
    all_to_all x1, waiting for transfers between devices, body(): lax.all_to_all(wide_values, 'seq', split_axis=1, concat_axis=0, tiled=True)  37.3 us
    another operation x4, loops' own time, attend_head(): result = lax.map(one_step, starts)  32.5 us
    gather x16, local copies, waits for them, and re-layouts, one_step(): slash_keys = key_blocks[safe_ids].reshape(per_step, -1, head_dim)  30.3 us
  transfers between devices with their start and end apart: 5, of which 5 were waited for; matrix products, arithmetic and copies ran while one was open for 3% of the time, Pallas kernels for 0%

commit v1 on v0

v1 whole, which is shorter than its diff:
```python
import functools
import math

import jax
import jax.numpy as jnp
from jax import lax
from jax.experimental import pallas as pl
from jax.experimental.pallas import tpu as pltpu
from jax.sharding import PartitionSpec as P

BLOCK = 64
QUAD = 4
LOG2E = 1.4426950408889634


def attend_block(q, block, first_head, head, offs_ref, vert_ref, w_s, c_s, lane_row, slashes, verts):
    row = first_head + head
    pieces = []
    for c in range(slashes):
        offset = offs_ref[row, c]
        pieces.append((w_s, jnp.maximum(block - offset, 0), offset))
    for c in range(verts):
        pieces.append((c_s, vert_ref[row, c], None))

    def rows(which, piece):
        ref, index, _ = piece
        return ref[which, index]

    factor = LOG2E / math.sqrt(q.shape[-1])
    chunks = [pieces[a : a + QUAD] for a in range(0, len(pieces), QUAD)]
    scores = []
    for chunk in chunks:
        keys = jnp.concatenate([rows(0, piece) for piece in chunk], axis=0)
        s = lax.dot_general(q, keys, (((1,), (1,)), ((), ())), preferred_element_type=jnp.float32)
        if any(piece[2] is not None for piece in chunk):
            lane = lax.broadcasted_iota(jnp.int32, (1, s.shape[1]), 1)
            offsets = jnp.full((1, s.shape[1]), -1, jnp.int32)
            for a, piece in enumerate(chunk):
                if piece[2] is not None:
                    offsets = jnp.where(lane // BLOCK == a, piece[2], offsets)
            limits = jnp.where(offsets > block, -4 * BLOCK, 4 * BLOCK)
            limits = jnp.where(offsets == 0, 0, limits)
            s = jnp.where(lane_row[:, : s.shape[1]] <= limits, s, -1e30)
        scores.append(s)
    top = functools.reduce(jnp.maximum, [jnp.max(s, axis=1, keepdims=True) for s in scores])
    total = None
    mixed = None
    for chunk, s in zip(chunks, scores):
        weights = jnp.exp2((s - top) * factor)
        part = jnp.sum(weights, axis=1, keepdims=True)
        values = jnp.concatenate([rows(1, piece) for piece in chunk], axis=0)
        product = jnp.dot(
            weights.astype(jnp.bfloat16), values, preferred_element_type=jnp.float32
        )
        total = part if total is None else total + part
        mixed = product if mixed is None else mixed + product
    return (mixed / total).astype(jnp.bfloat16)


def kernel(
    n, members, heads, slashes, verts,
    offs_ref, vert_ref, q_in, w_in, c_in, out,
    q_s, w_s, c_s, o_s,
    w_send, w_recv, c_send, c_recv, q_send, q_recv, o_send, o_recv, local_sem,
):
    me = lax.axis_index("seq")
    member = lax.rem(me, members)
    base = me - member
    span = q_in.shape[1]
    first_head = member * heads

    barrier = pltpu.get_barrier_semaphore()

    def greet(k, _):
        pl.semaphore_signal(
            barrier, inc=1, device_id={"seq": lax.rem(me + k, n)},
            device_id_type=pl.DeviceIdType.MESH,
        )
        return 0

    lax.fori_loop(1, n, greet, 0)

    def span_of(index, length):
        return pl.ds(pl.multiple_of(index * length, length), length)

    def blocks_of(index, ref):
        return pl.ds(index * ref.shape[2], ref.shape[2])

    own = [
        pltpu.make_async_copy(w_in.at[member], w_s.at[:, blocks_of(me, w_in)], local_sem.at[0]),
        pltpu.make_async_copy(c_in.at[member], c_s.at[:, blocks_of(me, c_in)], local_sem.at[1]),
        pltpu.make_async_copy(
            q_in.at[pl.ds(first_head, heads)], q_s.at[:, span_of(member, span), :], local_sem.at[2]
        ),
    ]
    for copy in own:
        copy.start()
    pl.semaphore_wait(barrier, n - 1)

    def remote(src, dst, send, recv, peer):
        return pltpu.make_async_remote_copy(
            src_ref=src, dst_ref=dst, send_sem=send, recv_sem=recv,
            device_id={"seq": peer}, device_id_type=pl.DeviceIdType.MESH,
        )

    def w_copy(peer, place):
        return remote(
            w_in.at[lax.rem(peer, members)], w_s.at[:, blocks_of(place, w_in)],
            w_send.at[peer], w_recv.at[place], peer,
        )

    def c_copy(peer, place):
        return remote(
            c_in.at[lax.rem(peer, members)], c_s.at[:, blocks_of(place, c_in)],
            c_send.at[peer], c_recv.at[place], peer,
        )

    def q_copy(head, peer, place):
        return remote(
            q_in.at[peer * heads + head], q_s.at[head, span_of(place, span), :],
            q_send.at[head, peer], q_recv.at[head, place], base + peer,
        )

    def o_copy(head, peer, place):
        return remote(
            o_s.at[head, span_of(peer, span), :], out.at[place * heads + head],
            o_send.at[head, peer], o_recv.at[head, place], base + peer,
        )

    def start_kv(k, _):
        peer = lax.rem(me + k, n)
        w_copy(peer, me).start()
        c_copy(peer, me).start()
        return 0

    lax.fori_loop(1, n, start_kv, 0)

    def start_q(step, _):
        head = step // (members - 1)
        peer = lax.rem(member + 1 + lax.rem(step, members - 1), members)
        q_copy(head, peer, member).start()
        return 0

    lax.fori_loop(0, heads * (members - 1), start_q, 0)

    for copy in own:
        copy.wait()

    def wait_kv(k, _):
        other = lax.rem(me + k, n)
        w_copy(other, other).wait_recv()
        c_copy(other, other).wait_recv()
        return 0

    lax.fori_loop(1, n, wait_kv, 0)

    lane_row = lax.rem(
        lax.broadcasted_iota(jnp.int32, (BLOCK, QUAD * BLOCK), 1), BLOCK
    ) - lax.broadcasted_iota(jnp.int32, (BLOCK, QUAD * BLOCK), 0)
    blocks = members * span // BLOCK
    first_block = (base * span) // BLOCK

    def one_head(head, _):
        def wait_q(k, _):
            other = lax.rem(member + k, members)
            q_copy(head, other, other).wait_recv()
            return 0

        lax.fori_loop(1, members, wait_q, 0)

        def one_block(step, _):
            for half in range(2):
                local = step * 2 + half
                place = pl.ds(pl.multiple_of(local * BLOCK, BLOCK), BLOCK)
                o_s[head, place, :] = attend_block(
                    q_s[head, place, :], first_block + local, first_head, head,
                    offs_ref, vert_ref, w_s, c_s, lane_row, slashes, verts,
                )
            return 0

        lax.fori_loop(0, blocks // 2, one_block, 0)

        def start_o(k, _):
            o_copy(head, lax.rem(member + k, members), member).start()
            return 0

        lax.fori_loop(1, members, start_o, 0)
        pltpu.make_async_copy(
            o_s.at[head, span_of(member, span), :], out.at[first_head + head],
            local_sem.at[3 + head],
        ).start()
        return 0

    lax.fori_loop(0, heads, one_head, 0)

    def finish_kv(k, _):
        peer = lax.rem(me + k, n)
        w_copy(peer, me).wait_send()
        c_copy(peer, me).wait_send()
        return 0

    lax.fori_loop(1, n, finish_kv, 0)

    def finish_head(head, _):
        def each(k, _):
            other = lax.rem(member + k, members)
            q_copy(head, other, member).wait_send()
            o_copy(head, other, member).wait_send()
            o_copy(head, other, other).wait_recv()
            return 0

        lax.fori_loop(1, members, each, 0)
        pltpu.make_async_copy(
            o_s.at[head, span_of(member, span), :], out.at[first_head + head],
            local_sem.at[3 + head],
        ).wait()
        return 0

    lax.fori_loop(0, heads, finish_head, 0)


def body(queries, window_keys, window_values, cache_keys, cache_values, vertical_blocks, slash_offsets):
    n = lax.axis_size("seq")
    span, head_count, dim = queries.shape
    members = window_keys.shape[1]
    cspan = cache_keys.shape[0]
    heads = head_count // members
    q_in = jnp.transpose(queries, (1, 0, 2))

    def by_head(keys, values):
        both = [jnp.transpose(a, (1, 0, 2)).reshape(members, -1, BLOCK, dim) for a in (keys, values)]
        return jnp.stack(both, axis=1)

    w_in = by_head(window_keys, window_values)
    c_in = by_head(cache_keys, cache_values)
    slashes, verts = slash_offsets.shape[1], vertical_blocks.shape[1]
    keys = (slashes + verts) * BLOCK
    any_spec = pl.BlockSpec(memory_space=pl.ANY)
    smem = pl.BlockSpec(memory_space=pltpu.SMEM)
    dma = pltpu.SemaphoreType.DMA
    out = pl.pallas_call(
        functools.partial(kernel, n, members, heads, slashes, verts),
        out_shape=jax.ShapeDtypeStruct((head_count, span, dim), jnp.bfloat16),
        in_specs=[smem, smem, any_spec, any_spec, any_spec],
        out_specs=any_spec,
        scratch_shapes=[
            pltpu.VMEM((heads, members * span, dim), jnp.bfloat16),
            pltpu.VMEM((2, n * span // BLOCK, BLOCK, dim), jnp.bfloat16),
            pltpu.VMEM((2, n * cspan // BLOCK, BLOCK, dim), jnp.bfloat16),
            pltpu.VMEM((heads, members * span, dim), jnp.bfloat16),
            dma((n,)), dma((n,)), dma((n,)), dma((n,)),
            dma((heads, members)), dma((heads, members)),
            dma((heads, members)), dma((heads, members)),
            dma((3 + heads,)),
        ],
        compiler_params=pltpu.CompilerParams(
            collective_id=0, has_side_effects=True, vmem_limit_bytes=48 * 1024 * 1024
        ),
        cost_estimate=pl.CostEstimate(
            flops=4 * heads * members * span * keys * dim,
            bytes_accessed=16 * heads * members * span * dim,
            transcendentals=heads * members * span * keys,
        ),
    )(slash_offsets, vertical_blocks, q_in, w_in, c_in)
    return jnp.transpose(out, (1, 0, 2))


def solution(mesh):
    rows = P(("grp", "seq"), None, None)
    placed = (rows, rows, rows, rows, rows, P("grp", None), P("grp", None))
    return jax.shard_map(body, mesh=mesh, in_specs=placed, out_specs=rows, check_vma=False)
```

time: 685 us -> 152 us (0.22)
  waiting for transfers between devices: 263 us -> 0 us
  local copies, waits for them, and re-layouts: 165 us -> 9.1 us
  Pallas kernels: 0 us -> 142 us
  matrix products: 68.9 us -> 0 us
  blocking collectives: 66.8 us -> 0 us
  starting transfers between devices: 59.6 us -> 0 us
  loops' own time: 32.5 us -> 0 us
  other arithmetic: 24.9 us -> 0.15 us
    all_to_all x5 -> x0, waiting for transfers between devices: 263 us -> none  [the longest x1 78 us: body(): lax.all_to_all(cache_wide_keys, 'seq', split_axis=1, concat_axis=0, tiled...]
    pallas_call x0 -> x1, Pallas kernels: none -> 142 us  [body(): pl.pallas_call(functools.partial(kernel, n, members, heads, slashes, vert...]
    dot_general x64 -> x0, matrix products: 68.9 us -> none  [the longest x16 26.8 us: one_step(): jnp.einsum('gqd,gkd->gqk', query_group, slash_keys, preferred_element_typ...]
    gather x34 -> x0, local copies, waits for them, and re-layouts: 67.5 us -> none  [the longest x16 30.3 us: one_step(): slash_keys = key_blocks[safe_ids].reshape(per_step, -1, head_dim)]
    all_to_all x1 -> x0, blocking collectives: 66.8 us -> none  [body(): lax.all_to_all(by_position, 'seq', split_axis=0, concat_axis=1, tiled=True)]
    all_to_all x5 -> x0, starting transfers between devices: 59.6 us -> none  [the longest x1 19.4 us: body(): lax.all_to_all(cache_wide_values, 'seq', split_axis=1, concat_axis=0, til...]
    another operation x5 -> x0, loops' own time: 32.5 us -> none  [the longest x4 32.5 us: attend_head(): result = lax.map(one_step, starts)]
    dynamic_slice x29 -> x0, local copies, waits for them, and re-layouts: 29.9 us -> none  [the longest x12 20.1 us: body(): outputs = lax.map(per_head, stacked)]
  transfers between devices with their start and end apart: 5 -> 0, of which waited for: 5 -> 0; matrix products, arithmetic and copies ran while one was open for 3% -> 0% of each run, Pallas kernels for 0% -> 0%
where the time goes in v1:
time: 152 us; the launch traced here: 151 us
  Pallas kernels  142 us (93%)
  local copies, waits for them, and re-layouts  9.1 us (6%)
    pallas_call x1, Pallas kernels, body(): pl.pallas_call(functools.partial(kernel, n, members, heads, slashes, vert...  142 us
    unnamed x9, local copies, waits for them, and re-layouts  4.31 us

profile of v1, /device:TPU:1, one launch (start us, length us, event | category | flops | bytes accessed | tf_op | source)
XLA Modules:
  0.0 151.1 jit_solution(12978585489560272642)
XLA Ops:
  0.0 0.0 copy-start.2
  0.0 0.0 copy-start.1
  0.0 0.9 copy.14.vert_ref
  0.9 0.8 copy.13.offs_ref
  1.6 1.0 copy.9
  2.6 1.0 copy.10
  3.6 0.1 pad_maximum_fusion.1.w_in
  3.7 0.0 copy-done.1
  3.7 0.0 copy-start
  3.7 0.1 copy.11
  3.8 0.0 copy-done.2
  3.8 0.1 copy.12
  3.9 0.1 pad_maximum_fusion.c_in
  4.0 1.3 copy-done
  5.3 1.4 copy.17
  6.6 141.8 %shard_map.73 = bf16[64,128,128]{2,1,0:T(8,128)(2,1)S(1)} custom-call(s32[64,12]{1,0:T(8,128)S(1)} %copy.13.offs_ref, s32[64,4]{1,0:T(8,128)S(1)} %copy.14.vert_ref, bf16[64,128,128]{2,1,0:T(8,128)(2,1)S(1)} %bitcast.13, bf16[8,2,2,64,128]{4,3,2,1,0:T(8,128)(2,1)S(1)} %pad_maximum_fusion.1.w_in, bf16[8,2,4,64,128]{4,3,2,1,0:T(8,128)(2,1)S(1)} %pad_maximum_fusion.c_in), custom_call_target="tpu_custom_call" | custom-call | flops 4294967296 | bytes 16777216 | tf_op jit(solution)/shard_map/pallas_call | solution.py:241
  148.4 2.7 %copy.15 = bf16[128,64,128]{2,1,0:T(8,128)(2,1)} copy(bf16[128,64,128]{2,0,1:T(8,128)(2,1)S(1)} %bitcast.12) | data formatting | bytes 4194304 | tf_op jit(solution)/shard_map/transpose | solution.py:265
Async XLA Ops:
  0.0 3.8 %copy-start.2 = (bf16[256,8,128]{2,1,0:T(8,128)(2,1)S(1)}, bf16[256,8,128]{2,1,0:T(8,128)(2,1)}, u32[]{:S(2)}) copy-start(bf16[256,8,128]{2,1,0:T(8,128)(2,1)} %param.11) | copy-start | bytes 1572868
  0.0 3.7 %copy-start.1 = (bf16[256,8,128]{2,1,0:T(8,128)(2,1)S(1)}, bf16[256,8,128]{2,1,0:T(8,128)(2,1)}, u32[]{:S(2)}) copy-start(bf16[256,8,128]{2,1,0:T(8,128)(2,1)} %param.10) | copy-start | bytes 1572868
  3.7 1.6 %copy-start = (bf16[128,64,128]{2,1,0:T(8,128)(2,1)S(1)}, bf16[128,64,128]{2,1,0:T(8,128)(2,1)}, u32[]{:S(2)}) copy-start(bf16[128,64,128]{2,1,0:T(8,128)(2,1)} %param.7) | copy-start | bytes 6291460

commit v2 on v1

--- a/solution.py
+++ b/solution.py
@@ -10,57 +10,46 @@
 
 BLOCK = 64
 QUAD = 4
+UNROLL = 4
 LOG2E = 1.4426950408889634
 
 
-def attend_block(q, block, first_head, head, offs_ref, vert_ref, w_s, c_s, lane_row, slashes, verts):
-    row = first_head + head
+def slash_part(q, block, row, offs_ref, w_s, lane_row, slashes, factor):
     pieces = []
     for c in range(slashes):
         offset = offs_ref[row, c]
-        pieces.append((w_s, jnp.maximum(block - offset, 0), offset))
-    for c in range(verts):
-        pieces.append((c_s, vert_ref[row, c], None))
-
-    def rows(which, piece):
-        ref, index, _ = piece
-        return ref[which, index]
-
-    factor = LOG2E / math.sqrt(q.shape[-1])
-    chunks = [pieces[a : a + QUAD] for a in range(0, len(pieces), QUAD)]
+        pieces.append((jnp.maximum(block - offset, 0), offset))
+    chunks = [pieces[a : a + QUAD] for a in range(0, slashes, QUAD)]
     scores = []
     for chunk in chunks:
-        keys = jnp.concatenate([rows(0, piece) for piece in chunk], axis=0)
+        keys = jnp.concatenate([w_s[0, index] for index, _ in chunk], axis=0)
         s = lax.dot_general(q, keys, (((1,), (1,)), ((), ())), preferred_element_type=jnp.float32)
-        if any(piece[2] is not None for piece in chunk):
-            lane = lax.broadcasted_iota(jnp.int32, (1, s.shape[1]), 1)
-            offsets = jnp.full((1, s.shape[1]), -1, jnp.int32)
-            for a, piece in enumerate(chunk):
-                if piece[2] is not None:
-                    offsets = jnp.where(lane // BLOCK == a, piece[2], offsets)
-            limits = jnp.where(offsets > block, -4 * BLOCK, 4 * BLOCK)
-            limits = jnp.where(offsets == 0, 0, limits)
-            s = jnp.where(lane_row[:, : s.shape[1]] <= limits, s, -1e30)
-        scores.append(s)
+        lane = lax.broadcasted_iota(jnp.int32, (1, s.shape[1]), 1)
+        offsets = jnp.full((1, s.shape[1]), -1, jnp.int32)
+        for a, (_, offset) in enumerate(chunk):
+            offsets = jnp.where(lane // BLOCK == a, offset, offsets)
+        limits = jnp.where(offsets > block, -4 * BLOCK, 4 * BLOCK)
+        limits = jnp.where(offsets == 0, 0, limits)
+        scores.append(jnp.where(lane_row[:, : s.shape[1]] <= limits, s, -1e30))
     top = functools.reduce(jnp.maximum, [jnp.max(s, axis=1, keepdims=True) for s in scores])
     total = None
     mixed = None
     for chunk, s in zip(chunks, scores):
         weights = jnp.exp2((s - top) * factor)
         part = jnp.sum(weights, axis=1, keepdims=True)
-        values = jnp.concatenate([rows(1, piece) for piece in chunk], axis=0)
+        values = jnp.concatenate([w_s[1, index] for index, _ in chunk], axis=0)
         product = jnp.dot(
             weights.astype(jnp.bfloat16), values, preferred_element_type=jnp.float32
         )
         total = part if total is None else total + part
         mixed = product if mixed is None else mixed + product
-    return (mixed / total).astype(jnp.bfloat16)
+    return top, total, mixed
 
 
 def kernel(
     n, members, heads, slashes, verts,
     offs_ref, vert_ref, q_in, w_in, c_in, out,
-    q_s, w_s, c_s, o_s,
+    q_s, w_s, c_s, o_s, top_s, total_s, mixed_s,
     w_send, w_recv, c_send, c_recv, q_send, q_recv, o_send, o_recv, local_sem,
 ):
     me = lax.axis_index("seq")
@@ -127,32 +116,40 @@
             o_send.at[head, peer], o_recv.at[head, place], base + peer,
         )
 
-    def start_kv(k, _):
-        peer = lax.rem(me + k, n)
-        w_copy(peer, me).start()
-        c_copy(peer, me).start()
-        return 0
-
-    lax.fori_loop(1, n, start_kv, 0)
-
-    def start_q(step, _):
-        head = step // (members - 1)
-        peer = lax.rem(member + 1 + lax.rem(step, members - 1), members)
-        q_copy(head, peer, member).start()
-        return 0
-
-    lax.fori_loop(0, heads * (members - 1), start_q, 0)
+    def start_w(k, _):
+        w_copy(lax.rem(me + k, n), me).start()
+        return 0
+
+    lax.fori_loop(1, n, start_w, 0)
+    share = -(-(n - 1) // heads)
+
+    def start_head(head, _):
+        def start_q(k, _):
+            q_copy(head, lax.rem(member + k, members), member).start()
+            return 0
+
+        def start_c(k, _):
+            @pl.when(k < n)
+            def _():
+                c_copy(lax.rem(me + k, n), me).start()
+
+            return 0
+
+        lax.fori_loop(1, members, start_q, 0)
+        lax.fori_loop(1 + head * share, 1 + (head + 1) * share, start_c, 0)
+        return 0
+
+    lax.fori_loop(0, heads, start_head, 0)
 
     for copy in own:
         copy.wait()
 
-    def wait_kv(k, _):
+    def wait_w(k, _):
         other = lax.rem(me + k, n)
         w_copy(other, other).wait_recv()
-        c_copy(other, other).wait_recv()
-        return 0
-
-    lax.fori_loop(1, n, wait_kv, 0)
+        return 0
+
+    lax.fori_loop(1, n, wait_w, 0)
 
     lane_row = lax.rem(
         lax.broadcasted_iota(jnp.int32, (BLOCK, QUAD * BLOCK), 1), BLOCK
@@ -160,7 +157,9 @@
     blocks = members * span // BLOCK
     first_block = (base * span) // BLOCK
 
-    def one_head(head, _):
+    factor = LOG2E / math.sqrt(q_s.shape[-1])
+
+    def slash_head(head, _):
         def wait_q(k, _):
             other = lax.rem(member + k, members)
             q_copy(head, other, other).wait_recv()
@@ -168,17 +167,53 @@
 
         lax.fori_loop(1, members, wait_q, 0)
 
-        def one_block(step, _):
-            for half in range(2):
-                local = step * 2 + half
+        def some_blocks(step, _):
+            for part in range(UNROLL):
+                local = step * UNROLL + part
                 place = pl.ds(pl.multiple_of(local * BLOCK, BLOCK), BLOCK)
-                o_s[head, place, :] = attend_block(
-                    q_s[head, place, :], first_block + local, first_head, head,
-                    offs_ref, vert_ref, w_s, c_s, lane_row, slashes, verts,
+                top, total, mixed = slash_part(
+                    q_s[head, place, :], first_block + local, first_head + head,
+                    offs_ref, w_s, lane_row, slashes, factor,
                 )
-            return 0
-
-        lax.fori_loop(0, blocks // 2, one_block, 0)
+                top_s[head, place, :] = jnp.broadcast_to(top, mixed.shape)
+                total_s[head, place, :] = jnp.broadcast_to(total, mixed.shape)
+                mixed_s[head, place, :] = mixed
+            return 0
+
+        lax.fori_loop(0, blocks // UNROLL, some_blocks, 0)
+        return 0
+
+    lax.fori_loop(0, heads, slash_head, 0)
+
+    def wait_c(k, _):
+        other = lax.rem(me + k, n)
+        c_copy(other, other).wait_recv()
+        return 0
+
+    lax.fori_loop(1, n, wait_c, 0)
+    tall = math.gcd(members * span, 4 * BLOCK)
+
+    def vertical_head(head, _):
+        row = first_head + head
+        picks = [vert_ref[row, c] for c in range(verts)]
+        keys = jnp.concatenate([c_s[0, pick] for pick in picks], axis=0)
+        values = jnp.concatenate([c_s[1, pick] for pick in picks], axis=0)
+        for step in range(members * span // tall):
+            place = pl.ds(step * tall, tall)
+            s = lax.dot_general(
+                q_s[head, place, :], keys, (((1,), (1,)), ((), ())),
+                preferred_element_type=jnp.float32,
+            )
+            before = top_s[head, place, :]
+            top = jnp.maximum(before, jnp.max(s, axis=1, keepdims=True))
+            scale = jnp.exp2((before - top) * factor)
+            weights = jnp.exp2((s - top[:, :1]) * factor)
+            total = total_s[head, place, :] * scale + jnp.sum(weights, axis=1, keepdims=True)
+            product = jnp.dot(
+                weights.astype(jnp.bfloat16), values, preferred_element_type=jnp.float32
+            )
+            mixed = mixed_s[head, place, :] * scale + product
+            o_s[head, place, :] = (mixed / total).astype(jnp.bfloat16)
 
         def start_o(k, _):
             o_copy(head, lax.rem(member + k, members), member).start()
@@ -191,7 +226,7 @@
         ).start()
         return 0
 
-    lax.fori_loop(0, heads, one_head, 0)
+    lax.fori_loop(0, heads, vertical_head, 0)
 
     def finish_kv(k, _):
         peer = lax.rem(me + k, n)
@@ -248,6 +283,9 @@
             pltpu.VMEM((2, n * span // BLOCK, BLOCK, dim), jnp.bfloat16),
             pltpu.VMEM((2, n * cspan // BLOCK, BLOCK, dim), jnp.bfloat16),
             pltpu.VMEM((heads, members * span, dim), jnp.bfloat16),
+            pltpu.VMEM((heads, members * span, dim), jnp.float32),
+            pltpu.VMEM((heads, members * span, dim), jnp.float32),
+            pltpu.VMEM((heads, members * span, dim), jnp.float32),
             dma((n,)), dma((n,)), dma((n,)), dma((n,)),
             dma((heads, members)), dma((heads, members)),
             dma((heads, members)), dma((heads, members)),

time: 152 us -> 128 us (0.84)
  Pallas kernels: 142 us -> 118 us
    pallas_call x1, Pallas kernels: 142 us -> 118 us  [body(): pl.pallas_call(functools.partial(kernel, n, members, heads, slashes, vert...]
where the time goes in v2:
time: 128 us
  Pallas kernels  118 us (92%)
  local copies, waits for them, and re-layouts  9.1 us (7%)
    pallas_call x1, Pallas kernels, body(): pl.pallas_call(functools.partial(kernel, n, members, heads, slashes, vert...  118 us
    unnamed x9, local copies, waits for them, and re-layouts  4.31 us
    transpose x1, local copies, waits for them, and re-layouts, body(): return jnp.transpose(out, (1, 0, 2))  2.67 us

profile of v2, /device:TPU:1, one launch (start us, length us, event | category | flops | bytes accessed | tf_op | source)
XLA Modules:
  0.0 127.6 jit_solution(17956710903203563094)
XLA Ops:
  0.0 0.0 copy-start.2
  0.0 0.0 copy-start.1
  0.0 0.9 copy.14.vert_ref
  0.9 0.8 copy.13.offs_ref
  1.6 1.0 copy.9
  2.6 1.0 copy.10
  3.6 0.1 pad_maximum_fusion.1.w_in
  3.7 0.0 copy-done.1
  3.7 0.0 copy-start
  3.7 0.1 copy.11
  3.8 0.0 copy-done.2
  3.8 0.1 copy.12
  3.9 0.1 pad_maximum_fusion.c_in
  4.0 1.3 %copy-done = bf16[128,64,128]{2,1,0:T(8,128)(2,1)S(1)} copy-done((bf16[128,64,128]{2,1,0:T(8,128)(2,1)S(1)}, bf16[128,64,128]{2,1,0:T(8,128)(2,1)}, u32[]{:S(2)}) %copy-start) | copy-done | bytes 2097176
  5.3 1.4 %copy.17 = bf16[128,64,128]{2,0,1:T(8,128)(2,1)S(1)} copy(bf16[128,64,128]{2,1,0:T(8,128)(2,1)S(1)} %copy-done) | data formatting | bytes 4194304 | tf_op args[0]
  6.6 118.3 %shard_map.73 = bf16[64,128,128]{2,1,0:T(8,128)(2,1)S(1)} custom-call(s32[64,12]{1,0:T(8,128)S(1)} %copy.13.offs_ref, s32[64,4]{1,0:T(8,128)S(1)} %copy.14.vert_ref, bf16[64,128,128]{2,1,0:T(8,128)(2,1)S(1)} %bitcast.13, bf16[8,2,2,64,128]{4,3,2,1,0:T(8,128)(2,1)S(1)} %pad_maximum_fusion.1.w_in, bf16[8,2,4,64,128]{4,3,2,1,0:T(8,128)(2,1)S(1)} %pad_maximum_fusion.c_in), custom_call_target="tpu_custom_call" | custom-call | flops 4294967296 | bytes 16777216 | tf_op jit(solution)/shard_map/pallas_call | solution.py:276
  125.0 2.7 %copy.15 = bf16[128,64,128]{2,1,0:T(8,128)(2,1)} copy(bf16[128,64,128]{2,0,1:T(8,128)(2,1)S(1)} %bitcast.12) | data formatting | bytes 4194304 | tf_op jit(solution)/shard_map/transpose | solution.py:303
Async XLA Ops:
  0.0 3.8 %copy-start.2 = (bf16[256,8,128]{2,1,0:T(8,128)(2,1)S(1)}, bf16[256,8,128]{2,1,0:T(8,128)(2,1)}, u32[]{:S(2)}) copy-start(bf16[256,8,128]{2,1,0:T(8,128)(2,1)} %param.11) | copy-start | bytes 1572868
  0.0 3.7 %copy-start.1 = (bf16[256,8,128]{2,1,0:T(8,128)(2,1)S(1)}, bf16[256,8,128]{2,1,0:T(8,128)(2,1)}, u32[]{:S(2)}) copy-start(bf16[256,8,128]{2,1,0:T(8,128)(2,1)} %param.10) | copy-start | bytes 1572868
  3.7 1.6 %copy-start = (bf16[128,64,128]{2,1,0:T(8,128)(2,1)S(1)}, bf16[128,64,128]{2,1,0:T(8,128)(2,1)}, u32[]{:S(2)}) copy-start(bf16[128,64,128]{2,1,0:T(8,128)(2,1)} %param.7) | copy-start | bytes 6291460

commit v3 on v2

--- a/solution.py
+++ b/solution.py
@@ -55,6 +55,7 @@
     me = lax.axis_index("seq")
     member = lax.rem(me, members)
     base = me - member
+    stride = 7 if math.gcd(7, n) == 1 else 1
     span = q_in.shape[1]
     first_head = member * heads
 
@@ -62,7 +63,7 @@
 
     def greet(k, _):
         pl.semaphore_signal(
-            barrier, inc=1, device_id={"seq": lax.rem(me + k, n)},
+            barrier, inc=1, device_id={"seq": lax.rem(me + k * stride, n)},
             device_id_type=pl.DeviceIdType.MESH,
         )
         return 0
@@ -117,10 +118,9 @@
         )
 
     def start_w(k, _):
-        w_copy(lax.rem(me + k, n), me).start()
-        return 0
-
-    lax.fori_loop(1, n, start_w, 0)
+        w_copy(lax.rem(me + k * stride, n), me).start()
+        return 0
+
     share = -(-(n - 1) // heads)
 
     def start_head(head, _):
@@ -131,21 +131,31 @@
         def start_c(k, _):
             @pl.when(k < n)
             def _():
-                c_copy(lax.rem(me + k, n), me).start()
-
+                c_copy(lax.rem(me + k * stride, n), me).start()
+
+            return 0
+
+        lax.fori_loop(1 + head * share, 1 + (head + 1) * share, start_c, 0)
+        return 0
+
+    lax.fori_loop(1, n, start_w, 0)
+
+    def start_qs(head, _):
+        def start_q(k, _):
+            q_copy(head, lax.rem(member + k, members), member).start()
             return 0
 
         lax.fori_loop(1, members, start_q, 0)
-        lax.fori_loop(1 + head * share, 1 + (head + 1) * share, start_c, 0)
-        return 0
-
+        return 0
+
+    lax.fori_loop(0, heads, start_qs, 0)
     lax.fori_loop(0, heads, start_head, 0)
 
     for copy in own:
         copy.wait()
 
     def wait_w(k, _):
-        other = lax.rem(me + k, n)
+        other = lax.rem(me + k * stride, n)
         w_copy(other, other).wait_recv()
         return 0
 
@@ -186,7 +196,7 @@
     lax.fori_loop(0, heads, slash_head, 0)
 
     def wait_c(k, _):
-        other = lax.rem(me + k, n)
+        other = lax.rem(me + k * stride, n)
         c_copy(other, other).wait_recv()
         return 0
 
@@ -229,7 +239,7 @@
     lax.fori_loop(0, heads, vertical_head, 0)
 
     def finish_kv(k, _):
-        peer = lax.rem(me + k, n)
+        peer = lax.rem(me + k * stride, n)
         w_copy(peer, me).wait_send()
         c_copy(peer, me).wait_send()
         return 0

time: 128 us -> 119 us (0.930)
  Pallas kernels: 118 us -> 110 us
    pallas_call x1, Pallas kernels: 118 us -> 110 us  [body(): pl.pallas_call(functools.partial(kernel, n, members, heads, slashes, vert...]
where the time goes in v3:
time: 119 us
  Pallas kernels  110 us (92%)
  local copies, waits for them, and re-layouts  9.1 us (8%)
    pallas_call x1, Pallas kernels, body(): pl.pallas_call(functools.partial(kernel, n, members, heads, slashes, vert...  110 us
    unnamed x9, local copies, waits for them, and re-layouts  4.31 us
    transpose x1, local copies, waits for them, and re-layouts, body(): return jnp.transpose(out, (1, 0, 2))  2.67 us

profile of v3, /device:TPU:1, one launch (start us, length us, event | category | flops | bytes accessed | tf_op | source)
XLA Modules:
  0.0 119.1 jit_solution(16469204621576450729)
XLA Ops:
  0.0 0.0 copy-start.2
  0.0 0.0 copy-start.1
  0.0 0.9 copy.14.vert_ref
  0.9 0.8 copy.13.offs_ref
  1.6 1.0 copy.9
  2.6 1.0 copy.10
  3.6 0.1 pad_maximum_fusion.1.w_in
  3.7 0.0 copy-done.1
  3.7 0.0 copy-start
  3.7 0.1 copy.11
  3.8 0.0 copy-done.2
  3.8 0.1 copy.12
  3.9 0.1 pad_maximum_fusion.c_in
  4.0 1.3 %copy-done = bf16[128,64,128]{2,1,0:T(8,128)(2,1)S(1)} copy-done((bf16[128,64,128]{2,1,0:T(8,128)(2,1)S(1)}, bf16[128,64,128]{2,1,0:T(8,128)(2,1)}, u32[]{:S(2)}) %copy-start) | copy-done | bytes 2097176
  5.3 1.4 %copy.17 = bf16[128,64,128]{2,0,1:T(8,128)(2,1)S(1)} copy(bf16[128,64,128]{2,1,0:T(8,128)(2,1)S(1)} %copy-done) | data formatting | bytes 4194304 | tf_op args[0]
  6.6 109.7 %shard_map.73 = bf16[64,128,128]{2,1,0:T(8,128)(2,1)S(1)} custom-call(s32[64,12]{1,0:T(8,128)S(1)} %copy.13.offs_ref, s32[64,4]{1,0:T(8,128)S(1)} %copy.14.vert_ref, bf16[64,128,128]{2,1,0:T(8,128)(2,1)S(1)} %bitcast.13, bf16[8,2,2,64,128]{4,3,2,1,0:T(8,128)(2,1)S(1)} %pad_maximum_fusion.1.w_in, bf16[8,2,4,64,128]{4,3,2,1,0:T(8,128)(2,1)S(1)} %pad_maximum_fusion.c_in), custom_call_target="tpu_custom_call" | custom-call | flops 4294967296 | bytes 16777216 | tf_op jit(solution)/shard_map/pallas_call | solution.py:286
  116.4 2.7 %copy.15 = bf16[128,64,128]{2,1,0:T(8,128)(2,1)} copy(bf16[128,64,128]{2,0,1:T(8,128)(2,1)S(1)} %bitcast.12) | data formatting | bytes 4194304 | tf_op jit(solution)/shard_map/transpose | solution.py:313
Async XLA Ops:
  0.0 3.8 %copy-start.2 = (bf16[256,8,128]{2,1,0:T(8,128)(2,1)S(1)}, bf16[256,8,128]{2,1,0:T(8,128)(2,1)}, u32[]{:S(2)}) copy-start(bf16[256,8,128]{2,1,0:T(8,128)(2,1)} %param.11) | copy-start | bytes 1572868
  0.0 3.7 %copy-start.1 = (bf16[256,8,128]{2,1,0:T(8,128)(2,1)S(1)}, bf16[256,8,128]{2,1,0:T(8,128)(2,1)}, u32[]{:S(2)}) copy-start(bf16[256,8,128]{2,1,0:T(8,128)(2,1)} %param.10) | copy-start | bytes 1572868
  3.7 1.6 %copy-start = (bf16[128,64,128]{2,1,0:T(8,128)(2,1)S(1)}, bf16[128,64,128]{2,1,0:T(8,128)(2,1)}, u32[]{:S(2)}) copy-start(bf16[128,64,128]{2,1,0:T(8,128)(2,1)} %param.7) | copy-start | bytes 6291460
